TPU v7x, 512 devices: a whole 4x8x8 slice. The times are simulated.
512 devices in a mesh: energy: 64 (over z, y), slab: 8 (over x, core).
Axes of the slice: x: 4, y: 8, z: 8, core: 2. Of those that a mesh axis runs over, the one named last changes fastest.
Arguments:
- lesser_free: float32 [128, 144, 1024], P('energy', None, 'slab'), may hold values from -6 to 6
- greater_free: float32 [128, 144, 1024], P('energy', None, 'slab'), may hold values from -6 to 6
- retarded: float32 [128, 144, 1024], P('energy', None, 'slab'), may hold values from -1.75 to 1.75
- coupling: float32 [12, 144, 1024], P(None, None, 'slab'), may hold values from -0.875 to 0.875
- neighbour_offsets: int32 [12, 1024], P(None, 'slab'), may hold values from -32 to 32, as said below
- phonon_shift: int32 [64], replicated, may hold values from 1 to 16, as said below
- phonon_coupling: float32 [64], replicated, may hold values from 0.01 to 0.1
- phonon_occupation: float32 [64], replicated, may hold values from 0.05 to 5
Outputs:
- green_lesser: float32 [128, 144, 1024], P('energy', None, 'slab')
- green_greater: float32 [128, 144, 1024], P('energy', None, 'slab')
Inputs may be any that keep to these rules, and one draw needn't show every extreme that they name: `neighbour_offsets`: each atom's 12 offsets are distinct and nonzero. `phonon_shift`: several frequencies may share a shift.
All inputs are finite; a program needn't handle non-finite values.
Results may differ from a plain program's by a relative error of at most 0.0003.
Values sent between devices are 32-bit elements; how exact they have to be, the bound alone decides.
A program may use at most 64 MiB of HBM per device.

v0:
```python
import jax
import jax.numpy as jnp
from jax import lax
from jax.sharding import PartitionSpec as P

NORB = 12
NB = 12
HW = 32
ITERS = 2


TOP_RANK = lax.Precision.HIGHEST


def padded_2(block, sides, width):
    for axis, dim in sides:
        count = lax.axis_size(axis)
        forward = [(i, i + 1) for i in range(count - 1)]
        backward = [(target, source) for source, target in forward]
        low = lax.ppermute(
            lax.slice_in_dim(block, block.shape[dim] - width, None, axis=dim), axis, forward
        )
        high = lax.ppermute(lax.slice_in_dim(block, 0, width, axis=dim), axis, backward)
        block = jnp.concatenate([low, block, high], axis=dim)
    return block


def banded(upper_weight, downward_weight, shifts, rows, column_entries, lead):
    length = rows + column_entries - 1
    spacing = jnp.arange(length, dtype=jnp.int32) - (rows - 1) - lead
    hits_upper = (spacing[None, :] == shifts[:, None]).astype(jnp.float32)
    hits_lower = (spacing[None, :] == -shifts[:, None]).astype(jnp.float32)
    coeffs = jnp.dot(upper_weight, hits_upper, precision=TOP_RANK) + jnp.dot(
        downward_weight, hits_lower, precision=TOP_RANK
    )
    tiled = jnp.concatenate([jnp.tile(coeffs, rows), jnp.zeros((rows,), jnp.float32)])
    hankel = tiled.reshape(rows, rows + column_entries)[:, :column_entries]
    return hankel[::-1]


def block_sandwich(left, middle):
    inner = 0.0
    for inner_index in range(left.shape[-2]):
        inner = inner + left[..., :, inner_index, None, :] * middle[..., None, inner_index, :, :]
    outer = 0.0
    for outer_index in range(left.shape[-2]):
        outer = outer + inner[..., :, None, outer_index, :] * left[..., None, :, outer_index, :]
    return outer


def couple(green, links, energy_displacements):
    atoms = green.shape[-1]
    padded = padded_2(green, (("slab", 4),), HW)
    wide = padded.shape[-1]
    padded_rows = padded.reshape(-1, wide)
    positions = jnp.arange(atoms, dtype=jnp.int32)
    sources = jnp.arange(wide, dtype=jnp.int32)

    def add_neighbour(neighbour, total):
        targets = positions + energy_displacements[neighbour] + HW
        selector = (sources[:, None] == targets[None, :]).astype(jnp.float32)
        near = jnp.dot(padded_rows, selector, precision=TOP_RANK).reshape(green.shape)
        return total + block_sandwich(links[neighbour], near)

    return lax.fori_loop(0, NB, add_neighbour, jnp.zeros(green.shape, jnp.float32))


def body(
    lesser_free,
    greater_free,
    retarded,
    coupling,
    neighbour_offsets,
    phonon_shift,
    phonon_coupling,
    phonon_occupation,
):
    energies, pairs, atoms = lesser_free.shape
    free = jnp.stack([lesser_free, greater_free]).reshape(2, energies, NORB, NORB, atoms)
    retarded_blocks = retarded.reshape(energies, NORB, NORB, atoms)
    links = coupling.reshape(NB, NORB, NORB, atoms)
    emit = phonon_coupling * (phonon_occupation + 1.0)
    absorb = phonon_coupling * phonon_occupation
    total_energies = energies * lax.axis_size("energy")
    kernel_stack = jnp.stack(
        [
            banded(emit, absorb, phonon_shift, total_energies, total_energies, 0),
            banded(absorb, emit, phonon_shift, total_energies, total_energies, 0),
        ]
    )
    green = free
    for step in range(ITERS):
        coupled = couple(green, links, neighbour_offsets)
        flat = coupled.reshape(2, energies, pairs * atoms)
        local_holdings = lax.all_to_all(flat, "energy", split_axis=2, concat_axis=1, tiled=True)
        blended_sigma = jnp.einsum("wah,whd->wad", kernel_stack, local_holdings, precision=TOP_RANK)
        sigma = lax.all_to_all(blended_sigma, "energy", split_axis=1, concat_axis=2, tiled=True)
        green = free + block_sandwich(
            retarded_blocks, sigma.reshape(2, energies, NORB, NORB, atoms)
        )
    result = green.reshape(2, energies, pairs, atoms)
    return (result[0], result[1])


def solution(mesh):
    placed = (
        P("energy", None, "slab"),
        P("energy", None, "slab"),
        P("energy", None, "slab"),
        P(None, None, "slab"),
        P(None, "slab"),
        P(),
        P(),
        P(),
    )
    return jax.shard_map(
        body,
        mesh=mesh,
        in_specs=placed,
        out_specs=(P("energy", None, "slab"), P("energy", None, "slab")),
        check_vma=False,
    )
```

profile of v0, /device:TPU:1, one launch (start us, length us, event | category | flops | bytes accessed | tf_op | source)
XLA Modules:
  0.0 368.6 jit_solution(12920151986132069248)
XLA Ops:
  0.6 1.0 copy.123
  1.6 1.0 copy.124
  2.6 1.2 fusion.18
  3.8 4.5 %collective-permute-start = (f32[2,2,12,12,32]{4,1,3,2,0:T(2,128)}, f32[2,2,12,12,32]{4,1,3,2,0:T(2,128)}, u32[]{:S(2)}, u32[]{:S(2)}) collective-permute-start(f32[2,2,12,12,32]{4,1,3,2,0:T(2,128)} %get-tuple-element.464), channel_id=1, source_target_pairs={{0,1},{1,2},{2,3},{3,4},{4,5},{5,6},{6,7},{8,9},{9,10},{10,11},{11... | collective-permute-start | bytes 221192 | tf_op jit(solution)/shard_map/ppermute | solution.py:20
  8.3 6.3 %collective-permute-start.1 = (f32[2,2,12,12,32]{4,1,3,2,0:T(2,128)S(1)}, f32[2,2,12,12,32]{4,1,3,2,0:T(2,128)}, u32[]{:S(2)}, u32[]{:S(2)}) collective-permute-start(f32[2,2,12,12,32]{4,1,3,2,0:T(2,128)S(1)} %get-tuple-element.465), channel_id=1, source_target_pairs={{1,0},{2,1},{3,2},{4,3},{5,4},{6,5},{7,6},{9,8},{10,9},{11,10},{12... | collective-permute-start | bytes 221192 | tf_op jit(solution)/shard_map/ppermute | solution.py:23
  14.6 0.9 fusion.24
  16.1 1.2 reshape.156
  17.7 2.0 pad_maximum_fusion
  19.7 1.0 copy.126
  20.7 1.2 reshape.157
  21.9 27.3 %while.28 = (s32[]{:T(128)}, f32[2,2,12,12,128]{4,3,2,1,0:T(8,128)S(1)}, f32[12,12,12,128]{3,1,2,0:T(8,128)S(1)}, s32[12,128]{1,0:T(8,128)}, f32[576,192]{1,0:T(8,128)S(1)}, /*index=5*/s32[]{:T(128)}, s32[]{:T(128)}) while((s32[]{:T(128)}, f32[2,2,12,12,128]{4,3,2,1,0:T(8,128)S(1)}, f32[12,12,12,128]{3,1,2,0:T(8,128)S(1)}, ...), condition=%wide.region_1.0_spmd.clone, body=%wide.region_0.0_spmd.clone.sunk | while | flops 173433088 | bytes 5015135 | solution.py:65
  21.9 0.7 fusion.47
  24.2 0.7 fusion.47
  26.5 0.7 fusion.47
  28.8 0.7 fusion.47
  31.0 0.7 fusion.47
  33.3 0.7 fusion.47
  35.6 0.7 fusion.47
  37.9 0.7 fusion.47
  40.1 0.7 fusion.47
  42.4 0.7 fusion.47
  44.7 0.7 fusion.47
  47.0 0.7 fusion.47
  49.3 16.5 %copy.168 = f32[2,2,12,12,128]{1,0,4,3,2:T(2,128)} copy(f32[2,2,12,12,128]{4,3,2,1,0:T(8,128)S(1)} %get-tuple-element.250) | data formatting | bytes 589824 | tf_op jit(solution)/shard_map/reshape | solution.py:94
  65.8 22.9 %reshape.175 = f32[64,1,1152]{2,1,0:T(1,128)} reshape(f32[18432,2,2]{2,1,0:T(2,128)} %bitcast.349) | data formatting | bytes 589824
  88.7 15.2 %all-to-all-start = ((f32[64,1,1152]{2,1,0:T(1,128)}), f32[64,1,1152]{2,1,0:T(1,128)S(1)}, u32[]{:S(2)}, u32[]{:S(2)}) async-start(f32[64,1,1152]{2,1,0:T(1,128)} %reshape.175), calls=%async_computation | async-start | bytes 589824 | tf_op jit(solution)/shard_map/all_to_all | solution.py:95
  105.5 11.1 %all-to-all-done = f32[64,1,1152]{2,1,0:T(1,128)S(1)} async-done(((f32[64,1,1152]{2,1,0:T(1,128)}), f32[64,1,1152]{2,1,0:T(1,128)S(1)}, u32[]{:S(2)}, u32[]{:S(2)}) %all-to-all-start) | async-done | bytes 294944 | tf_op jit(solution)/shard_map/all_to_all | solution.py:95
  117.0 1.3 reduce
  118.4 29.5 %reshape.176 = f32[18432,2,2]{2,1,0:T(2,128)} reshape(f32[64,1152]{1,0:T(8,128)S(1)} %reduce) | data formatting | bytes 589824
  147.9 18.6 %copy.169 = f32[2,2,64,288]{3,2,1,0:T(8,128)S(1)} copy(f32[2,2,64,288]{1,0,3,2:T(2,128)} %bitcast.350) | data formatting | bytes 589824 | tf_op jit(solution)/shard_map/all_to_all | solution.py:95
  166.9 0.8 fusion.16
  167.7 0.9 copy.132
  168.6 4.6 %all-to-all-start.1 = ((f32[2,128,288]{2,0,1:T(2,128)}), f32[2,128,288]{2,0,1:T(2,128)S(1)}, u32[]{:S(2)}, u32[]{:S(2)}) async-start(f32[2,128,288]{2,0,1:T(2,128)} %copy.132), calls=%async_computation.1 | async-start | bytes 786432 | tf_op jit(solution)/shard_map/all_to_all | solution.py:97
  173.4 15.0 %all-to-all-done.1 = f32[2,128,288]{2,0,1:T(2,128)S(1)} async-done(((f32[2,128,288]{2,0,1:T(2,128)}), f32[2,128,288]{2,0,1:T(2,128)S(1)}, u32[]{:S(2)}, u32[]{:S(2)}) %all-to-all-start.1) | async-done | bytes 294944 | tf_op jit(solution)/shard_map/all_to_all | solution.py:97
  189.0 0.9 multiply_add_fusion.3
  189.9 1.0 add_add_fusion.1
  191.3 7.5 %collective-permute-start.2 = (f32[2,2,12,12,32]{4,1,3,2,0:T(2,128)S(1)}, f32[2,2,12,12,32]{4,1,3,2,0:T(2,128)S(1)}, u32[]{:S(2)}, u32[]{:S(2)}) collective-permute-start(f32[2,2,12,12,32]{4,1,3,2,0:T(2,128)S(1)} %get-tuple-element.450), channel_id=1, source_target_pairs={{0,1},{1,2},{2,3},{3,4},{4,5},{5,6},{6,7},{8,9},{9,10},{10,11},{11... | collective-permute-start | bytes 221192 | tf_op jit(solution)/shard_map/ppermute | solution.py:20
  198.8 2.1 collective-permute-start.3
  201.0 1.5 collective-permute-done.2
  202.4 4.5 %collective-permute-done.3 = f32[2,2,12,12,32]{4,1,3,2,0:T(2,128)} collective-permute-done((f32[2,2,12,12,32]{4,1,3,2,0:T(2,128)S(1)}, f32[2,2,12,12,32]{4,1,3,2,0:T(2,128)}, u32[]{:S(2)}, u32[]{:S(2)}) %collective-permute-start.3) | collective-permute-done | bytes 73760 | tf_op jit(solution)/shard_map/ppermute | solution.py:23
  206.9 1.9 pad_maximum_fusion.1
  208.9 1.0 copy.146
  209.9 1.2 reshape.160
  211.1 27.3 %while.29 = (s32[]{:T(128)}, f32[2,2,12,12,128]{4,3,2,1,0:T(8,128)S(1)}, f32[12,12,12,128]{3,1,2,0:T(8,128)S(1)}, s32[12,128]{1,0:T(8,128)}, f32[576,192]{1,0:T(8,128)S(1)}, /*index=5*/s32[]{:T(128)}, s32[]{:T(128)}) while((s32[]{:T(128)}, f32[2,2,12,12,128]{4,3,2,1,0:T(8,128)S(1)}, f32[12,12,12,128]{3,1,2,0:T(8,128)S(1)}, ...), condition=%wide.region_3.0_spmd.clone, body=%wide.region_2.0_spmd.clone.sunk | while | flops 173433088 | bytes 5015135 | solution.py:65
  211.1 0.7 fusion.49
  213.4 0.7 fusion.49
  215.6 0.7 fusion.49
  217.9 0.7 fusion.49
  220.2 0.7 fusion.49
  222.5 0.7 fusion.49
  224.7 0.7 fusion.49
  229.3 0.7 fusion.49
  231.6 0.7 fusion.49
  233.9 0.7 fusion.49
  238.4 16.5 %copy.170 = f32[2,2,12,12,128]{1,0,4,3,2:T(2,128)} copy(f32[2,2,12,12,128]{4,3,2,1,0:T(8,128)S(1)} %get-tuple-element.251) | data formatting | bytes 589824 | tf_op jit(solution)/shard_map/reshape | solution.py:94
  254.9 22.2 %reshape.177 = f32[64,1,1152]{2,1,0:T(1,128)S(1)} reshape(f32[18432,2,2]{2,1,0:T(2,128)} %bitcast.351) | data formatting | bytes 589824
  277.2 17.6 %all_to_all.66 = f32[64,1,1152]{2,1,0:T(1,128)S(1)} all-to-all(f32[64,1,1152]{2,1,0:T(1,128)S(1)} %reshape.177), channel_id=1, replica_groups=mesh['energy'=64,'slab'=8] {'energy'}, dimensions={0} | all-to-all | bytes 589824 | tf_op jit(solution)/shard_map/all_to_all | solution.py:95
  294.7 1.3 reduce.1
  296.1 29.5 %reshape.178 = f32[18432,2,2]{2,1,0:T(2,128)} reshape(f32[64,1152]{1,0:T(8,128)S(1)} %reduce.1) | data formatting | bytes 589824
  325.6 18.6 %copy.171 = f32[2,2,64,288]{3,2,1,0:T(8,128)S(1)} copy(f32[2,2,64,288]{1,0,3,2:T(2,128)} %bitcast.352) | data formatting | bytes 589824 | tf_op jit(solution)/shard_map/all_to_all | solution.py:95
  344.6 0.8 fusion.14
  345.5 19.1 %all_to_all.67 = f32[2,128,288]{2,0,1:T(2,128)S(1)} all-to-all(f32[2,128,288]{2,0,1:T(2,128)S(1)} %copy.152), channel_id=1, replica_groups=mesh['energy'=64,'slab'=8] {'energy'}, dimensions={1} | all-to-all | bytes 589824 | tf_op jit(solution)/shard_map/all_to_all | solution.py:97
  365.3 0.9 multiply_add_fusion.2
  366.2 1.0 add_add_fusion
  (556 shorter events, 42.1 us)
Async XLA Ops:
  3.8 13.9 %collective-permute-start = (f32[2,2,12,12,32]{4,1,3,2,0:T(2,128)}, f32[2,2,12,12,32]{4,1,3,2,0:T(2,128)}, u32[]{:S(2)}, u32[]{:S(2)}) collective-permute-start(f32[2,2,12,12,32]{4,1,3,2,0:T(2,128)} %get-tuple-element.464), channel_id=1, source_target_pairs={{0,1},{1,2},{2,3},{3,4},{4,5},{5,6},{6,7},{8,9},{9,10},{10,11},{11... | collective-permute-start | bytes 221192 | tf_op jit(solution)/shard_map/ppermute | solution.py:20
  8.3 9.4 %collective-permute-start.1 = (f32[2,2,12,12,32]{4,1,3,2,0:T(2,128)S(1)}, f32[2,2,12,12,32]{4,1,3,2,0:T(2,128)}, u32[]{:S(2)}, u32[]{:S(2)}) collective-permute-start(f32[2,2,12,12,32]{4,1,3,2,0:T(2,128)S(1)} %get-tuple-element.465), channel_id=1, source_target_pairs={{1,0},{2,1},{3,2},{4,3},{5,4},{6,5},{7,6},{9,8},{10,9},{11,10},{12... | collective-permute-start | bytes 221192 | tf_op jit(solution)/shard_map/ppermute | solution.py:23
  49.2 54.7 %copy-start.2 = (f32[64]{0:T(128)S(1)}, f32[64]{0:T(128)}, u32[]{:S(2)}) copy-start(f32[64]{0:T(128)} %param.18) | copy-start | bytes 772
  49.3 54.7 %copy-start.3 = (f32[64]{0:T(128)S(1)}, f32[64]{0:T(128)}, u32[]{:S(2)}) copy-start(f32[64]{0:T(128)} %param.19) | copy-start | bytes 772
  49.3 55.5 %copy-start.1 = (s32[64]{0:T(128)S(1)}, s32[64]{0:T(128)}, u32[]{:S(2)}) copy-start(s32[64]{0:T(128)} %param.17) | copy-start | bytes 772
  88.7 27.8 %all-to-all-start = ((f32[64,1,1152]{2,1,0:T(1,128)}), f32[64,1,1152]{2,1,0:T(1,128)S(1)}, u32[]{:S(2)}, u32[]{:S(2)}) async-start(f32[64,1,1152]{2,1,0:T(1,128)} %reshape.175), calls=%async_computation | async-start | bytes 589824 | tf_op jit(solution)/shard_map/all_to_all | solution.py:95
  118.4 54.8 %copy-start = (f32[2,144,128]{2,1,0:T(8,128)S(1)}, f32[2,144,128]{2,1,0:T(8,128)}, u32[]{:S(2)}) copy-start(f32[2,144,128]{2,1,0:T(8,128)} %param.14) | copy-start | bytes 442372
  168.6 19.8 %all-to-all-start.1 = ((f32[2,128,288]{2,0,1:T(2,128)}), f32[2,128,288]{2,0,1:T(2,128)S(1)}, u32[]{:S(2)}, u32[]{:S(2)}) async-start(f32[2,128,288]{2,0,1:T(2,128)} %copy.132), calls=%async_computation.1 | async-start | bytes 786432 | tf_op jit(solution)/shard_map/all_to_all | solution.py:97
  191.3 11.2 %collective-permute-start.2 = (f32[2,2,12,12,32]{4,1,3,2,0:T(2,128)S(1)}, f32[2,2,12,12,32]{4,1,3,2,0:T(2,128)S(1)}, u32[]{:S(2)}, u32[]{:S(2)}) collective-permute-start(f32[2,2,12,12,32]{4,1,3,2,0:T(2,128)S(1)} %get-tuple-element.450), channel_id=1, source_target_pairs={{0,1},{1,2},{2,3},{3,4},{4,5},{5,6},{6,7},{8,9},{9,10},{10,11},{11... | collective-permute-start | bytes 221192 | tf_op jit(solution)/shard_map/ppermute | solution.py:20
  198.8 8.1 %collective-permute-start.3 = (f32[2,2,12,12,32]{4,1,3,2,0:T(2,128)S(1)}, f32[2,2,12,12,32]{4,1,3,2,0:T(2,128)}, u32[]{:S(2)}, u32[]{:S(2)}) collective-permute-start(f32[2,2,12,12,32]{4,1,3,2,0:T(2,128)S(1)} %get-tuple-element.451), channel_id=1, source_target_pairs={{1,0},{2,1},{3,2},{4,3},{5,4},{6,5},{7,6},{9,8},{10,9},{11,10},{12... | collective-permute-start | bytes 221192 | tf_op jit(solution)/shard_map/ppermute | solution.py:23
where the time goes:
time: 375 us; the launch traced here: 369 us
  local copies, waits for them, and re-layouts  195 us (52%)
  other arithmetic  46 us (12%)
  starting transfers between devices  40.3 us (11%)
  blocking collectives  36.6 us (10%)
  waiting for transfers between devices  32 us (9%)
  matrix products  13 us (3%)
  loops' own time  3.98 us (1%)
    unnamed x18, local copies, waits for them, and re-layouts  108 us
    all_to_all x5, local copies, waits for them, and re-layouts, body(): lax.all_to_all(flat, 'energy', split_axis=2, concat_axis=1, tiled=True)  38.4 us
    reshape x2, local copies, waits for them, and re-layouts, body(): flat = coupled.reshape(2, energies, pairs * atoms)  33.1 us
    all_to_all x1, blocking collectives, body(): lax.all_to_all(blended_sigma, 'energy', split_axis=1, concat_axis=2, tile...  19.1 us
    all_to_all x1, blocking collectives, body(): lax.all_to_all(flat, 'energy', split_axis=2, concat_axis=1, tiled=True)  17.6 us
    eq x24, other arithmetic, add_neighbour(): selector = (sources[:, None] == targets[None, :]).astype(jnp.float32)  16.7 us
    all_to_all x1, starting transfers between devices, body(): lax.all_to_all(flat, 'energy', split_axis=2, concat_axis=1, tiled=True)  15.2 us
    all_to_all x1, waiting for transfers between devices, body(): lax.all_to_all(blended_sigma, 'energy', split_axis=1, concat_axis=2, tile...  15 us
  transfers between devices with their start and end apart: 6, of which 4 were waited for; matrix products, arithmetic and copies ran while one was open for 1% of the time, Pallas kernels for 0%

commit v1 on v0

v1 whole, which is shorter than its diff:
```python
import functools

import jax
import jax.numpy as jnp
from jax import lax
from jax.experimental import pallas as pl
from jax.experimental.pallas import tpu as pltpu
from jax.sharding import PartitionSpec as P

NORB = 12
NB = 12
ITERS = 2
RING = 8
PAIRS = NORB * NORB
ROWS = 2 * PAIRS
PIECE = 40
PADDED = RING * PIECE
LANES = 128
MESH = pl.DeviceIdType.MESH


def spread(row):
    return jnp.broadcast_to(row, (8, LANES))


def rows8(start):
    return pl.ds(start, 8)


def gather_row(own, halo, near, inside, index, v):
    a = jnp.take_along_axis(own[rows8(8 * v), :], index, axis=1, mode="promise_in_bounds")
    h = jnp.take_along_axis(halo[rows8(8 * v), :], index, axis=1, mode="promise_in_bounds")
    near[v] = jnp.where(inside, a, h)


def gather_index(offsets, n):
    place = lax.broadcasted_iota(jnp.int32, (8, LANES), 1) + spread(offsets[pl.ds(n, 1), :])
    inside = (place >= 0) & (place < LANES)
    return inside, place & (LANES - 1)


def sandwich_step(n, links, wide_links, near, total, fetch):
    inner = [[None] * 3 for _ in range(NORB)]
    for j in range(NORB):
        block = [near[3 * j + l] for l in range(3)]
        for l in range(3):
            fetch(3 * j + l)
        for i in range(NORB):
            factor = spread(links[n, pl.ds(i * NORB + j, 1), :])
            for l in range(3):
                term = factor * block[l]
                inner[i][l] = term if j == 0 else inner[i][l] + term
    for k in range(NORB):
        start = n * ROWS
        right = [wide_links[rows8(pl.multiple_of(start + 8 * (3 * k + l), 8)), :] for l in range(3)]
        for i in range(NORB):
            term = inner[i][0] * right[0] + inner[i][1] * right[1] + inner[i][2] * right[2]
            total[i * NORB + k] += term


def fold(parts):
    sub = lax.broadcasted_iota(jnp.int32, (8, LANES), 0)
    low = sub < 4
    even = (sub & 2) == 0

    def halves(a, b):
        return jnp.where(low, a, b) + pltpu.roll(jnp.where(low, b, a), 4, 0)

    first = halves(parts[0], parts[2])
    second = halves(parts[1], parts[3])
    other = jnp.where(even, second, first)
    moved = jnp.where(even, pltpu.roll(first, 6, 0), pltpu.roll(second, 2, 0))
    del other
    return jnp.where(even, first, second) + moved


def dress(sigma, free, target, narrow, wide):
    inner = [[None] * 3 for _ in range(NORB)]
    for j in range(NORB):
        block = [sigma[rows8(8 * (3 * j + l)), :] for l in range(3)]
        for i in range(NORB):
            factor = narrow[i * NORB + j]
            for l in range(3):
                term = factor * block[l]
                inner[i][l] = term if j == 0 else inner[i][l] + term
    for i in range(NORB):
        for k3 in range(3):
            parts = []
            for q in range(4):
                k = 4 * k3 + q
                right = [wide[rows8(8 * (3 * k + l)), :] for l in range(3)]
                parts.append(inner[i][0] * right[0] + inner[i][1] * right[1] + inner[i][2] * right[2])
            at = 8 * (3 * i + k3)
            target[rows8(at), :] = free[rows8(at), :] + fold(parts)


def hop(m):
    half = (m + 1) // 2
    return 4 + half * (2 * (m % 2) - 1)


def kernel(
    lesser, greater, retarded, coupling, offsets, shifts, strength, occupation,
    out_lesser, out_greater,
    free_in, ret_in, links, wide_links, narrow_ret, wide_ret, taps, even_taps, odd_taps,
    lesser_buf, greater_buf, coupled, arrived, mixed, band, left_in, right_in,
    near_a, near_b, halo, total, sigma,
    load_sem, a1_send, a1_recv, z_send, z_recv, a2_send, a2_recv, x_send, x_recv,
):
    energy = lax.axis_index("energy")
    slab = lax.axis_index("slab")
    z = energy // RING
    y = energy % RING
    slabs = lax.axis_size("slab")
    planes = lax.axis_size("energy") // RING
    above = ((z + 1) % planes) * RING + y
    below = ((z + planes - 1) % planes) * RING + y
    right = (slab + 1) % slabs
    left = (slab + slabs - 1) % slabs

    loads = [
        pltpu.make_async_copy(lesser, free_in.at[0], load_sem.at[0]),
        pltpu.make_async_copy(greater, free_in.at[1], load_sem.at[1]),
        pltpu.make_async_copy(retarded, ret_in, load_sem.at[2]),
        pltpu.make_async_copy(coupling, links, load_sem.at[3]),
    ]
    for load in loads:
        load.start()

    barrier = pltpu.get_barrier_semaphore()

    def greet(m, carry):
        pl.semaphore_signal(
            barrier, inc=1, device_id=(z * RING + (y + hop(m)) % RING, slab), device_id_type=MESH
        )
        return carry

    lax.fori_loop(0, RING - 1, greet, 0)
    for peer in ((above, slab), (below, slab), (energy, right), (energy, left)):
        pl.semaphore_signal(barrier, inc=1, device_id=peer, device_id_type=MESH)

    def source(kind, t):
        return lesser_buf.at[t] if kind == 0 else coupled.at[t]

    def remote(src, dst, send, recv, peer):
        return pltpu.make_async_remote_copy(
            src_ref=src, dst_ref=dst, send_sem=send, recv_sem=recv, device_id=peer, device_id_type=MESH
        )

    def await_bytes(ref, sem):
        pltpu.make_async_copy(ref, ref, sem).wait()

    def piece(index):
        return pl.ds(pl.multiple_of(index * PIECE, 8), PIECE)

    def spread_start(kind, t):
        held = source(kind, t)

        def send(m, carry):
            to = (y + hop(m)) % RING
            remote(
                held.at[piece(to)], band.at[kind, t, piece(RING + y)],
                a1_send.at[kind, t, m], a1_recv.at[kind, t, m], (z * RING + to, slab),
            ).start()
            return carry

        pltpu.make_async_copy(
            held.at[piece(y)], band.at[kind, t, piece(RING + y)], a1_recv.at[kind, t, RING - 1]
        ).start()
        lax.fori_loop(0, RING - 1, send, 0)

    def spread_forward(kind, t):
        def pass_on(s, carry):
            m = (s + RING - 1) % RING
            origin = (y + RING - hop(m) * (1 - m // (RING - 1))) % RING
            here = band.at[kind, t, piece(RING + origin)]
            await_bytes(here, a1_recv.at[kind, t, m])
            remote(
                here, band.at[kind, t, piece(origin)],
                z_send.at[kind, t, 0, m], z_recv.at[kind, t, 0, m], (above, slab),
            ).start()
            remote(
                here, band.at[kind, t, piece(2 * RING + origin)],
                z_send.at[kind, t, 1, m], z_recv.at[kind, t, 1, m], (below, slab),
            ).start()
            return carry

        lax.fori_loop(0, RING, pass_on, 0)

    def mix(kind, t):
        def arrive(m, carry):
            for side in range(2):
                await_bytes(band.at[kind, t, piece(0)], z_recv.at[kind, t, side, m])
            return carry

        lax.fori_loop(0, RING, arrive, 0)

        @pl.when(z == 0)
        def _():
            band[kind, t, pl.ds(0, PADDED), :] = jnp.zeros((PADDED, LANES), jnp.float32)

        @pl.when(z == planes - 1)
        def _():
            band[kind, t, pl.ds(2 * PADDED, PADDED), :] = jnp.zeros((PADDED, LANES), jnp.float32)

        odd = (lax.broadcasted_iota(jnp.int32, (8, LANES), 0) & 1) == 1

        def blend(m, carry):
            to = (y + hop(m) * (1 - m // (RING - 1))) % RING
            tiles = PIECE // 8
            same = [None] * tiles
            swap = [None] * tiles
            for d in range(2 * RING + 1):
                first = odd_taps[kind, d]
                second = even_taps[kind, d]
                for r in range(tiles):
                    value = band[kind, t, rows8(pl.multiple_of((to + d) * PIECE + 8 * r, 8)), :]
                    term = value * first
                    swap[r] = term if d == 0 else swap[r] + term
                    if d != RING:
                        term = value * second
                        same[r] = term if d == 0 else same[r] + term
            for r in range(tiles):
                other = jnp.where(odd, pltpu.roll(swap[r], 1, 0), pltpu.roll(swap[r], 7, 0))
                mixed[kind, t, rows8(pl.multiple_of(m * PIECE + 8 * r, 8)), :] = same[r] + other

            @pl.when(m < RING - 1)
            def _():
                remote(
                    mixed.at[kind, t, piece(m)], arrived.at[kind, t, piece(y)],
                    a2_send.at[kind, t, m], a2_recv.at[kind, t, m], (z * RING + to, slab),
                ).start()

            @pl.when(m == RING - 1)
            def _():
                pltpu.make_async_copy(
                    mixed.at[kind, t, piece(m)], arrived.at[kind, t, piece(y)], a2_recv.at[kind, t, m]
                ).start()

            return carry

        lax.fori_loop(0, RING, blend, 0)

    def collect(kind, t, forward):
        def take(m, carry):
            origin = (y + RING - hop(m) * (1 - m // (RING - 1))) % RING
            here = arrived.at[kind, t, piece(origin)]
            await_bytes(here, a2_recv.at[kind, t, m])
            if forward:
                remote(
                    here, left_in.at[kind, t, piece(origin)],
                    x_send.at[kind, t, 0, m], x_recv.at[kind, t, 0, m], (energy, right),
                ).start()
                remote(
                    here, right_in.at[kind, t, piece(origin)],
                    x_send.at[kind, t, 1, m], x_recv.at[kind, t, 1, m], (energy, left),
                ).start()
            return carry

        lax.fori_loop(0, RING, take, 0)

    def edges_start(t):
        here = greater_buf.at[t]
        remote(here, left_in.at[1, t], x_send.at[1, t, 0, 0], x_recv.at[1, t, 0, 0], (energy, right)).start()
        remote(here, right_in.at[1, t], x_send.at[1, t, 1, 0], x_recv.at[1, t, 1, 0], (energy, left)).start()

    lane = lax.broadcasted_iota(jnp.int32, (8, LANES), 1)
    low_lanes = lane < LANES // 2
    edge_ok = jnp.where(low_lanes, slabs - 1 - slab, slab) > 0

    def edges_finish(kind, t):
        if kind == 1:
            await_bytes(left_in.at[1, t], x_recv.at[1, t, 0, 0])
            await_bytes(right_in.at[1, t], x_recv.at[1, t, 1, 0])
        else:
            def arrive(m, carry):
                for side in range(2):
                    await_bytes(left_in.at[0, t, piece(0)], x_recv.at[0, t, side, m])
                return carry

            lax.fori_loop(0, RING, arrive, 0)
        for v in range(ROWS // 8):
            value = jnp.where(low_lanes, right_in[kind, t, rows8(8 * v), :], left_in[kind, t, rows8(8 * v), :])
            halo[rows8(8 * v), :] = jnp.where(edge_ok, value, 0.0)

    def couple_first(own):
        inside, index = gather_index(offsets, 0)
        for v in range(ROWS // 8):
            gather_row(own, halo, near_a, inside, index, v)
        total[...] = jnp.zeros(total.shape, jnp.float32)

    def couple_part(own, begin, end):
        def step(h, carry):
            n = 2 * h
            inside, index = gather_index(offsets, n + 1)
            sandwich_step(
                n, links, wide_links, near_a, total,
                lambda v: gather_row(own, halo, near_b, inside, index, v),
            )
            inside_b, index_b = gather_index(offsets, (n + 2) % NB)
            sandwich_step(
                n + 1, links, wide_links, near_b, total,
                lambda v: gather_row(own, halo, near_a, inside_b, index_b, v),
            )
            return carry

        lax.fori_loop(begin, end, step, 0)

    def couple_last(target):
        for i in range(NORB):
            for k3 in range(3):
                target[rows8(8 * (3 * i + k3)), :] = fold([total[i * NORB + 4 * k3 + q] for q in range(4)])

    def interleave(kind, target):
        for e in range(2):
            for v in range(PAIRS // 8):
                target[pl.ds(16 * v + e, 8, stride=2), :] = free_in[kind, e, rows8(8 * v), :]

    zeros = jnp.zeros((PADDED - ROWS, LANES), jnp.float32)

    loads[0].wait()
    interleave(0, lesser_buf.at[0])
    for t in range(ITERS):
        lesser_buf[t, pl.ds(ROWS, PADDED - ROWS), :] = zeros
        greater_buf[t, pl.ds(ROWS, PADDED - ROWS), :] = zeros
        coupled[t, pl.ds(ROWS, PADDED - ROWS), :] = zeros
    pl.semaphore_wait(barrier, RING + 3)
    spread_start(0, 0)
    loads[1].wait()
    interleave(1, greater_buf.at[0])
    edges_start(0)

    row = lax.broadcasted_iota(jnp.int32, (PIECE, shifts.shape[1]), 0) - 17
    up = row == shifts[...]
    down = row == -shifts[...]
    emit = strength[...] * (occupation[...] + 1.0)
    absorb = strength[...] * occupation[...]
    for kind, (high, low) in enumerate(((emit, absorb), (absorb, emit))):
        column = jnp.sum(jnp.where(up, high, 0.0) + jnp.where(down, low, 0.0), axis=1, keepdims=True)
        taps[kind] = jnp.broadcast_to(column, (PIECE, LANES))
    odd_row = (lax.broadcasted_iota(jnp.int32, (8, LANES), 0) & 1) == 1
    for kind in range(2):
        for d in range(2 * RING + 1):
            even_taps[kind, d] = spread(taps[kind, pl.ds(2 * d + 1, 1), :])
            odd_taps[kind, d] = jnp.where(
                odd_row, spread(taps[kind, pl.ds(2 * d + 2, 1), :]), spread(taps[kind, pl.ds(2 * d, 1), :])
            )

    loads[2].wait()
    for r in range(PAIRS):
        narrow_ret[r] = jnp.where(odd_row, spread(ret_in[1, pl.ds(r, 1), :]), spread(ret_in[0, pl.ds(r, 1), :]))
    for e in range(2):
        for v in range(PAIRS // 8):
            wide_ret[pl.ds(16 * v + e, 8, stride=2), :] = ret_in[e, rows8(8 * v), :]
    loads[3].wait()

    def widen(n, carry):
        for v in range(PAIRS // 8):
            value = links[n, rows8(8 * v), :]
            for e in range(2):
                wide_links[pl.ds(n * ROWS + 16 * v + e, 8, stride=2), :] = value
        return carry

    lax.fori_loop(0, NB, widen, 0)

    def iteration(t, carry):
        spread_forward(0, t)
        edges_finish(1, t)
        own = greater_buf.at[t]
        couple_first(own)
        couple_part(own, 0, 3)
        mix(0, t)
        couple_part(own, 3, 6)
        couple_last(coupled.at[t])
        spread_start(1, t)
        collect(0, t, True)
        spread_forward(1, t)
        edges_finish(0, t)
        own = arrived.at[0, t]
        couple_first(own)
        couple_part(own, 0, 3)
        mix(1, t)
        couple_part(own, 3, 6)
        couple_last(sigma)
        dress(sigma, lesser_buf.at[0], lesser_buf.at[t + 1], narrow_ret, wide_ret)

        @pl.when(t < ITERS - 1)
        def _():
            spread_start(0, t + 1)

        collect(1, t, False)
        dress(arrived.at[1, t], greater_buf.at[0], greater_buf.at[t + 1], narrow_ret, wide_ret)

        @pl.when(t < ITERS - 1)
        def _():
            edges_start(t + 1)

        return carry

    lax.fori_loop(0, ITERS, iteration, 0)

    for e in range(2):
        for v in range(PAIRS // 8):
            out_lesser[e, rows8(8 * v), :] = lesser_buf[ITERS, pl.ds(16 * v + e, 8, stride=2), :]
            out_greater[e, rows8(8 * v), :] = greater_buf[ITERS, pl.ds(16 * v + e, 8, stride=2), :]

    def drain(t, carry):
        def pieces(m, inner):
            for kind in range(2):
                here = band.at[kind, t, piece(RING)]
                for side in range(2):
                    await_bytes(here, z_send.at[kind, t, side, m])

            for side in range(2):
                await_bytes(arrived.at[0, t, piece(0)], x_send.at[0, t, side, m])
            return inner

        def sent(m, inner):
            for kind in range(2):
                await_bytes(band.at[kind, t, piece(RING)], a1_send.at[kind, t, m])
                await_bytes(mixed.at[kind, t, piece(0)], a2_send.at[kind, t, m])
            return inner

        lax.fori_loop(0, RING, pieces, 0)
        lax.fori_loop(0, RING - 1, sent, 0)
        for side in range(2):
            await_bytes(greater_buf.at[t], x_send.at[1, t, side, 0])
        return carry

    lax.fori_loop(0, ITERS, drain, 0)


def body(lesser, greater, retarded, coupling, offsets, shifts, strength, occupation):
    f32 = jnp.float32
    vmem = functools.partial(pl.BlockSpec, memory_space=pltpu.VMEM)
    anywhere = functools.partial(pl.BlockSpec, memory_space=pl.ANY)
    lanes = lesser.shape[-1]
    dma = pltpu.SemaphoreType.DMA
    return pl.pallas_call(
        kernel,
        out_shape=(jax.ShapeDtypeStruct(lesser.shape, f32),) * 2,
        in_specs=[anywhere()] * 4 + [vmem()] * 4,
        out_specs=(vmem(), vmem()),
        scratch_shapes=[
            pltpu.VMEM((2, 2, PAIRS, lanes), f32),
            pltpu.VMEM((2, PAIRS, lanes), f32),
            pltpu.VMEM((NB, PAIRS, lanes), f32),
            pltpu.VMEM((NB * ROWS, lanes), f32),
            pltpu.VMEM((PAIRS, 8, lanes), f32),
            pltpu.VMEM((ROWS, lanes), f32),
            pltpu.VMEM((2, PIECE, lanes), f32),
            pltpu.VMEM((2, 2 * RING + 1, 8, lanes), f32),
            pltpu.VMEM((2, 2 * RING + 1, 8, lanes), f32),
            pltpu.VMEM((ITERS + 1, PADDED, lanes), f32),
            pltpu.VMEM((ITERS + 1, PADDED, lanes), f32),
            pltpu.VMEM((ITERS, PADDED, lanes), f32),
            pltpu.VMEM((2, ITERS, PADDED, lanes), f32),
            pltpu.VMEM((2, ITERS, PADDED, lanes), f32),
            pltpu.VMEM((2, ITERS, 3 * PADDED, lanes), f32),
            pltpu.VMEM((2, ITERS, PADDED, lanes), f32),
            pltpu.VMEM((2, ITERS, PADDED, lanes), f32),
            pltpu.VMEM((ROWS // 8, 8, lanes), f32),
            pltpu.VMEM((ROWS // 8, 8, lanes), f32),
            pltpu.VMEM((ROWS, lanes), f32),
            pltpu.VMEM((PAIRS, 8, lanes), f32),
            pltpu.VMEM((ROWS, lanes), f32),
            dma((4,)),
            dma((2, ITERS, RING - 1)),
            dma((2, ITERS, RING)),
            dma((2, ITERS, 2, RING)),
            dma((2, ITERS, 2, RING)),
            dma((2, ITERS, RING - 1)),
            dma((2, ITERS, RING)),
            dma((2, ITERS, 2, RING)),
            dma((2, ITERS, 2, RING)),
        ],
        compiler_params=pltpu.CompilerParams(
            collective_id=0, has_side_effects=True, vmem_limit_bytes=40 * 1024 * 1024
        ),
    )(
        lesser, greater, retarded, coupling, offsets,
        shifts.reshape(1, -1), strength.reshape(1, -1), occupation.reshape(1, -1),
    )


def solution(mesh):
    placed = (
        P("energy", None, "slab"),
        P("energy", None, "slab"),
        P("energy", None, "slab"),
        P(None, None, "slab"),
        P(None, "slab"),
        P(),
        P(),
        P(),
    )
    return jax.shard_map(
        body,
        mesh=mesh,
        in_specs=placed,
        out_specs=(P("energy", None, "slab"), P("energy", None, "slab")),
        check_vma=False,
    )
```

time: 375 us -> 83.3 us (0.22); the launches traced: 369 us -> 82.6 us
  local copies, waits for them, and re-layouts: 195 us -> 6.58 us
  Pallas kernels: 0 us -> 75.3 us
  other arithmetic: 46 us -> 0 us
  starting transfers between devices: 40.3 us -> 0 us
  blocking collectives: 36.6 us -> 0 us
  waiting for transfers between devices: 32 us -> 0 us
  matrix products: 13 us -> 0 us
  loops' own time: 3.98 us -> 0 us
    unnamed x18, local copies, waits for them, and re-layouts: 108 us -> 6.58 us
    pallas_call x0 -> x1, Pallas kernels: none -> 75.3 us  [body(): pl.pallas_call(kernel, out_shape=(jax.ShapeDtypeStruct(lesser.shape, f32)...]
    all_to_all x7 -> x0, local copies, waits for them, and re-layouts: 38.5 us -> none  [the longest x5 38.4 us: body(): lax.all_to_all(flat, 'energy', split_axis=2, concat_axis=1, tiled=True)]
    reshape x33 -> x0, local copies, waits for them, and re-layouts: 38 us -> none  [the longest x2 33.1 us: body(): flat = coupled.reshape(2, energies, pairs * atoms)]
    all_to_all x2 -> x0, blocking collectives: 36.6 us -> none  [the longest x1 19.1 us: body(): lax.all_to_all(blended_sigma, 'energy', split_axis=1, concat_axis=2, tile...]
    all_to_all x2 -> x0, waiting for transfers between devices: 26 us -> none  [the longest x1 15 us: body(): lax.all_to_all(blended_sigma, 'energy', split_axis=1, concat_axis=2, tile...]
    add x54 -> x0, other arithmetic: 20.7 us -> none  [the longest x26 9.51 us: block_sandwich(): inner + left[..., :, inner_index, None, :] * middle[..., None, inner_inde...]
    ppermute x4 -> x0, starting transfers between devices: 20.4 us -> none  [the longest x2 12 us: padded_2(): lax.ppermute(lax.slice_in_dim(block, block.shape[dim] - width, None, axis...]
  transfers between devices with their start and end apart: 6 -> 0, of which waited for: 4 -> 0; matrix products, arithmetic and copies ran while one was open for 1% -> 0% of each run, Pallas kernels for 0% -> 0%
where the time goes in v1:
time: 83.3 us; the launch traced here: 82.6 us
  Pallas kernels  75.3 us (90%)
  local copies, waits for them, and re-layouts  6.58 us (8%)
    pallas_call x1, Pallas kernels, body(): pl.pallas_call(kernel, out_shape=(jax.ShapeDtypeStruct(lesser.shape, f32)...  75.3 us
    unnamed x18, local copies, waits for them, and re-layouts  6.58 us

profile of v1, /device:TPU:1, one launch (start us, length us, event | category | flops | bytes accessed | tf_op | source)
XLA Modules:
  0.0 82.6 jit_solution(13205512447276076808)
XLA Ops:
  0.6 0.0 copy-start.5
  0.6 0.0 copy-start.6
  0.7 0.0 copy-start.7
  0.7 0.6 copy-done.5
  1.3 0.0 copy-done.6
  1.3 0.0 copy-done.7
  1.3 0.0 copy-start
  1.3 1.2 %copy-done = f32[12,144,128]{2,1,0:T(8,128)S(1)} copy-done((f32[12,144,128]{2,1,0:T(8,128)S(1)}, f32[12,144,128]{2,1,0:T(8,128)}, u32[]{:S(2)}) %copy-start) | copy-done | bytes 884760
  2.5 0.0 copy-start.1
  2.5 0.9 %copy-done.1 = f32[2,144,128]{2,1,0:T(8,128)S(1)} copy-done((f32[2,144,128]{2,1,0:T(8,128)S(1)}, f32[2,144,128]{2,1,0:T(8,128)}, u32[]{:S(2)}) %copy-start.1) | copy-done | bytes 147480
  3.4 0.0 copy-start.2
  3.4 0.9 %copy-done.2 = f32[2,144,128]{2,1,0:T(8,128)S(1)} copy-done((f32[2,144,128]{2,1,0:T(8,128)S(1)}, f32[2,144,128]{2,1,0:T(8,128)}, u32[]{:S(2)}) %copy-start.2) | copy-done | bytes 147480
  4.3 0.0 copy-start.3
  4.3 0.9 %copy-done.3 = f32[2,144,128]{2,1,0:T(8,128)S(1)} copy-done((f32[2,144,128]{2,1,0:T(8,128)S(1)}, f32[2,144,128]{2,1,0:T(8,128)}, u32[]{:S(2)}) %copy-start.3) | copy-done | bytes 147480
  5.2 0.0 copy-start.4
  5.2 0.7 copy-done.4
  5.9 75.3 %shard_map.95 = (f32[2,144,128]{2,1,0:T(8,128)S(1)}, f32[2,144,128]{2,1,0:T(8,128)S(1)}) custom-call(f32[2,144,128]{2,1,0:T(8,128)S(1)} %copy-done.1, f32[2,144,128]{2,1,0:T(8,128)S(1)} %copy-done.2, f32[2,144,128]{2,1,0:T(8,128)S(1)} %copy-done.3, f32[12,144,128]{2,1,0:T(8,128)S(1)} %copy-done, s32[12,128]{1,0:T(8,128)S(1)} %copy-done.4, ...), custom_call_target="tpu_custom_call" | custom-call | tf_op jit(solution)/shard_map/pallas_call | solution.py:439
  81.3 0.7 copy.12
  81.9 0.7 copy.13
Async XLA Ops:
  0.6 0.7 copy-start.5
  0.6 0.7 copy-start.6
  0.7 0.7 copy-start.7
  1.3 1.2 %copy-start = (f32[12,144,128]{2,1,0:T(8,128)S(1)}, f32[12,144,128]{2,1,0:T(8,128)}, u32[]{:S(2)}) copy-start(f32[12,144,128]{2,1,0:T(8,128)} %coupling.1) | copy-start | bytes 2654212
  2.5 0.9 %copy-start.1 = (f32[2,144,128]{2,1,0:T(8,128)S(1)}, f32[2,144,128]{2,1,0:T(8,128)}, u32[]{:S(2)}) copy-start(f32[2,144,128]{2,1,0:T(8,128)} %lesser.1) | copy-start | bytes 442372
  3.4 0.9 %copy-start.2 = (f32[2,144,128]{2,1,0:T(8,128)S(1)}, f32[2,144,128]{2,1,0:T(8,128)}, u32[]{:S(2)}) copy-start(f32[2,144,128]{2,1,0:T(8,128)} %greater.1) | copy-start | bytes 442372
  4.3 0.9 %copy-start.3 = (f32[2,144,128]{2,1,0:T(8,128)S(1)}, f32[2,144,128]{2,1,0:T(8,128)}, u32[]{:S(2)}) copy-start(f32[2,144,128]{2,1,0:T(8,128)} %retarded.1) | copy-start | bytes 442372
  5.2 0.7 copy-start.4

commit v2 on v1

--- a/solution.py
+++ b/solution.py
@@ -27,24 +27,14 @@
     return pl.ds(start, 8)
 
 
-def gather_row(own, halo, near, inside, index, v):
-    a = jnp.take_along_axis(own[rows8(8 * v), :], index, axis=1, mode="promise_in_bounds")
-    h = jnp.take_along_axis(halo[rows8(8 * v), :], index, axis=1, mode="promise_in_bounds")
-    near[v] = jnp.where(inside, a, h)
-
-
-def gather_index(offsets, n):
-    place = lax.broadcasted_iota(jnp.int32, (8, LANES), 1) + spread(offsets[pl.ds(n, 1), :])
-    inside = (place >= 0) & (place < LANES)
-    return inside, place & (LANES - 1)
-
-
-def sandwich_step(n, links, wide_links, near, total, fetch):
+def pick(source, v, index):
+    return jnp.take_along_axis(source[rows8(8 * v), :], index, axis=1, mode="promise_in_bounds")
+
+
+def sandwich_step(n, links, wide_links, near, total):
     inner = [[None] * 3 for _ in range(NORB)]
     for j in range(NORB):
-        block = [near[3 * j + l] for l in range(3)]
-        for l in range(3):
-            fetch(3 * j + l)
+        block = [near[n, 3 * j + l] for l in range(3)]
         for i in range(NORB):
             factor = spread(links[n, pl.ds(i * NORB + j, 1), :])
             for l in range(3):
@@ -100,11 +90,11 @@
 
 
 def kernel(
-    lesser, greater, retarded, coupling, offsets, shifts, strength, occupation,
+    lesser, greater, retarded, coupling, offsets_in, shifts_in, strength_in, occupation_in,
     out_lesser, out_greater,
-    free_in, ret_in, links, wide_links, narrow_ret, wide_ret, taps, even_taps, odd_taps,
+    offsets, shifts, strength, occupation, free_in, ret_in, links, wide_links, narrow_ret, wide_ret, taps, even_taps, odd_taps,
     lesser_buf, greater_buf, coupled, arrived, mixed, band, left_in, right_in,
-    near_a, near_b, halo, total, sigma,
+    pair_links, wide_pairs, stash, halo, total, sigma,
     load_sem, a1_send, a1_recv, z_send, z_recv, a2_send, a2_recv, x_send, x_recv,
 ):
     energy = lax.axis_index("energy")
@@ -123,10 +113,11 @@
         pltpu.make_async_copy(greater, free_in.at[1], load_sem.at[1]),
         pltpu.make_async_copy(retarded, ret_in, load_sem.at[2]),
         pltpu.make_async_copy(coupling, links, load_sem.at[3]),
+        pltpu.make_async_copy(offsets_in, offsets, load_sem.at[4]),
+        pltpu.make_async_copy(shifts_in, shifts, load_sem.at[5]),
+        pltpu.make_async_copy(strength_in, strength, load_sem.at[6]),
+        pltpu.make_async_copy(occupation_in, occupation, load_sem.at[7]),
     ]
-    for load in loads:
-        load.start()
-
     barrier = pltpu.get_barrier_semaphore()
 
     def greet(m, carry):
@@ -138,6 +129,8 @@
     lax.fori_loop(0, RING - 1, greet, 0)
     for peer in ((above, slab), (below, slab), (energy, right), (energy, left)):
         pl.semaphore_signal(barrier, inc=1, device_id=peer, device_id_type=MESH)
+    for load in loads:
+        load.start()
 
     def source(kind, t):
         return lesser_buf.at[t] if kind == 0 else coupled.at[t]
@@ -168,24 +161,29 @@
             held.at[piece(y)], band.at[kind, t, piece(RING + y)], a1_recv.at[kind, t, RING - 1]
         ).start()
         lax.fori_loop(0, RING - 1, send, 0)
+        pass_on(kind, t, RING - 1, y)
+
+    def pass_on(kind, t, m, origin):
+        here = band.at[kind, t, piece(RING + origin)]
+        await_bytes(here, a1_recv.at[kind, t, m])
+        remote(
+            here, band.at[kind, t, piece(origin)],
+            z_send.at[kind, t, 0, m], z_recv.at[kind, t, 0, m], (above, slab),
+        ).start()
+        remote(
+            here, band.at[kind, t, piece(2 * RING + origin)],
+            z_send.at[kind, t, 1, m], z_recv.at[kind, t, 1, m], (below, slab),
+        ).start()
+
+    def pass_near(kind, t, m):
+        pass_on(kind, t, m, (y + RING - hop(m)) % RING)
 
     def spread_forward(kind, t):
-        def pass_on(s, carry):
-            m = (s + RING - 1) % RING
-            origin = (y + RING - hop(m) * (1 - m // (RING - 1))) % RING
-            here = band.at[kind, t, piece(RING + origin)]
-            await_bytes(here, a1_recv.at[kind, t, m])
-            remote(
-                here, band.at[kind, t, piece(origin)],
-                z_send.at[kind, t, 0, m], z_recv.at[kind, t, 0, m], (above, slab),
-            ).start()
-            remote(
-                here, band.at[kind, t, piece(2 * RING + origin)],
-                z_send.at[kind, t, 1, m], z_recv.at[kind, t, 1, m], (below, slab),
-            ).start()
-            return carry
-
-        lax.fori_loop(0, RING, pass_on, 0)
+        def one(m, carry):
+            pass_near(kind, t, m)
+            return carry
+
+        lax.fori_loop(0, RING - 1, one, 0)
 
     def mix(kind, t):
         def arrive(m, carry):
@@ -267,6 +265,10 @@
     lane = lax.broadcasted_iota(jnp.int32, (8, LANES), 1)
     low_lanes = lane < LANES // 2
     edge_ok = jnp.where(low_lanes, slabs - 1 - slab, slab) > 0
+    outer = (lane < LANES // 4) | (lane >= LANES - LANES // 4)
+
+    def half_turn(value):
+        return pltpu.roll(value, LANES // 2, 1)
 
     def edges_finish(kind, t):
         if kind == 1:
@@ -281,35 +283,61 @@
             lax.fori_loop(0, RING, arrive, 0)
         for v in range(ROWS // 8):
             value = jnp.where(low_lanes, right_in[kind, t, rows8(8 * v), :], left_in[kind, t, rows8(8 * v), :])
-            halo[rows8(8 * v), :] = jnp.where(edge_ok, value, 0.0)
-
-    def couple_first(own):
-        inside, index = gather_index(offsets, 0)
-        for v in range(ROWS // 8):
-            gather_row(own, halo, near_a, inside, index, v)
+            value = jnp.where(edge_ok, value, 0.0)
+            halo[rows8(8 * v), :] = jnp.where(outer, value, half_turn(value))
+
+    def couple_own(own):
+        def one(n, carry):
+            place = lane + spread(offsets[pl.ds(n, 1), :])
+            inside = (place >= 0) & (place < LANES)
+            index = place & (LANES - 1)
+            for v in range(ROWS // 8):
+                stash[n, v] = jnp.where(inside, pick(own, v, index), 0.0)
+            return carry
+
+        lax.fori_loop(0, NB, one, 0)
         total[...] = jnp.zeros(total.shape, jnp.float32)
 
-    def couple_part(own, begin, end):
-        def step(h, carry):
-            n = 2 * h
-            inside, index = gather_index(offsets, n + 1)
-            sandwich_step(
-                n, links, wide_links, near_a, total,
-                lambda v: gather_row(own, halo, near_b, inside, index, v),
-            )
-            inside_b, index_b = gather_index(offsets, (n + 2) % NB)
-            sandwich_step(
-                n + 1, links, wide_links, near_b, total,
-                lambda v: gather_row(own, halo, near_a, inside_b, index_b, v),
-            )
+    def couple_steps(begin, end):
+        def step(n, carry):
+            sandwich_step(n, links, wide_links, stash, total)
             return carry
 
         lax.fori_loop(begin, end, step, 0)
 
-    def couple_last(target):
+    def folded(i, k3):
+        return fold([total[i * NORB + 4 * k3 + q] for q in range(4)])
+
+    def couple_inner(target):
         for i in range(NORB):
             for k3 in range(3):
-                target[rows8(8 * (3 * i + k3)), :] = fold([total[i * NORB + 4 * k3 + q] for q in range(4)])
+                target[rows8(8 * (3 * i + k3)), :] = folded(i, k3)
+
+    def couple_halo(target):
+        def one(h, carry):
+            near = spread(offsets[pl.ds(2 * h, 1), :])
+            far = spread(offsets[pl.ds(2 * h + 1, 1), :])
+            atom = jnp.where(outer, lane, lane ^ (LANES // 2))
+            place = atom + jnp.where(outer, near, half_turn(far))
+            beyond = (place < 0) | (place >= LANES)
+            index = (place + jnp.where(outer, 0, LANES // 2)) & (LANES - 1)
+            for v in range(ROWS // 8):
+                stash[h, v] = jnp.where(beyond, pick(halo, v, index), 0.0)
+            return carry
+
+        lax.fori_loop(0, NB // 2, one, 0)
+        total[...] = jnp.zeros(total.shape, jnp.float32)
+
+        def step(h, carry):
+            sandwich_step(h, pair_links, wide_pairs, stash, total)
+            return carry
+
+        lax.fori_loop(0, NB // 2, step, 0)
+        for i in range(NORB):
+            for k3 in range(3):
+                at = rows8(8 * (3 * i + k3))
+                value = folded(i, k3)
+                target[at, :] += jnp.where(outer, value + half_turn(value), 0.0)
 
     def interleave(kind, target):
         for e in range(2):
@@ -320,16 +348,19 @@
 
     loads[0].wait()
     interleave(0, lesser_buf.at[0])
+    loads[1].wait()
+    interleave(1, greater_buf.at[0])
     for t in range(ITERS):
         lesser_buf[t, pl.ds(ROWS, PADDED - ROWS), :] = zeros
         greater_buf[t, pl.ds(ROWS, PADDED - ROWS), :] = zeros
         coupled[t, pl.ds(ROWS, PADDED - ROWS), :] = zeros
+
     pl.semaphore_wait(barrier, RING + 3)
     spread_start(0, 0)
-    loads[1].wait()
-    interleave(1, greater_buf.at[0])
     edges_start(0)
 
+    for load in loads[4:]:
+        load.wait()
     row = lax.broadcasted_iota(jnp.int32, (PIECE, shifts.shape[1]), 0) - 17
     up = row == shifts[...]
     down = row == -shifts[...]
@@ -363,25 +394,34 @@
 
     lax.fori_loop(0, NB, widen, 0)
 
+    def widen_pair(h, carry):
+        for v in range(PAIRS // 8):
+            value = jnp.where(outer, links[2 * h, rows8(8 * v), :], half_turn(links[2 * h + 1, rows8(8 * v), :]))
+            pair_links[h, rows8(8 * v), :] = value
+            for e in range(2):
+                wide_pairs[pl.ds(h * ROWS + 16 * v + e, 8, stride=2), :] = value
+        return carry
+
+    lax.fori_loop(0, NB // 2, widen_pair, 0)
+    couple_own(greater_buf.at[0])
+    couple_steps(0, NB)
+    couple_inner(coupled.at[0])
+
     def iteration(t, carry):
         spread_forward(0, t)
         edges_finish(1, t)
-        own = greater_buf.at[t]
-        couple_first(own)
-        couple_part(own, 0, 3)
+        couple_halo(coupled.at[t])
+        spread_start(1, t)
         mix(0, t)
-        couple_part(own, 3, 6)
-        couple_last(coupled.at[t])
-        spread_start(1, t)
+        spread_forward(1, t)
         collect(0, t, True)
-        spread_forward(1, t)
+        couple_own(arrived.at[0, t])
+        couple_steps(0, NB // 2)
+        mix(1, t)
+        couple_steps(NB // 2, NB)
+        couple_inner(sigma)
         edges_finish(0, t)
-        own = arrived.at[0, t]
-        couple_first(own)
-        couple_part(own, 0, 3)
-        mix(1, t)
-        couple_part(own, 3, 6)
-        couple_last(sigma)
+        couple_halo(sigma)
         dress(sigma, lesser_buf.at[0], lesser_buf.at[t + 1], narrow_ret, wide_ret)
 
         @pl.when(t < ITERS - 1)
@@ -394,6 +434,9 @@
         @pl.when(t < ITERS - 1)
         def _():
             edges_start(t + 1)
+            couple_own(greater_buf.at[t + 1])
+            couple_steps(0, NB)
+            couple_inner(coupled.at[t + 1])
 
         return carry
 
@@ -433,15 +476,19 @@
 def body(lesser, greater, retarded, coupling, offsets, shifts, strength, occupation):
     f32 = jnp.float32
     vmem = functools.partial(pl.BlockSpec, memory_space=pltpu.VMEM)
-    anywhere = functools.partial(pl.BlockSpec, memory_space=pl.ANY)
+    outside = functools.partial(pl.BlockSpec, memory_space=pltpu.HBM)
     lanes = lesser.shape[-1]
     dma = pltpu.SemaphoreType.DMA
     return pl.pallas_call(
         kernel,
         out_shape=(jax.ShapeDtypeStruct(lesser.shape, f32),) * 2,
-        in_specs=[anywhere()] * 4 + [vmem()] * 4,
+        in_specs=[outside()] * 8,
         out_specs=(vmem(), vmem()),
         scratch_shapes=[
+            pltpu.VMEM(offsets.shape, jnp.int32),
+            pltpu.VMEM((1, shifts.shape[0]), jnp.int32),
+            pltpu.VMEM((1, shifts.shape[0]), f32),
+            pltpu.VMEM((1, shifts.shape[0]), f32),
             pltpu.VMEM((2, 2, PAIRS, lanes), f32),
             pltpu.VMEM((2, PAIRS, lanes), f32),
             pltpu.VMEM((NB, PAIRS, lanes), f32),
@@ -459,12 +506,13 @@
             pltpu.VMEM((2, ITERS, 3 * PADDED, lanes), f32),
             pltpu.VMEM((2, ITERS, PADDED, lanes), f32),
             pltpu.VMEM((2, ITERS, PADDED, lanes), f32),
-            pltpu.VMEM((ROWS // 8, 8, lanes), f32),
-            pltpu.VMEM((ROWS // 8, 8, lanes), f32),
+            pltpu.VMEM((NB // 2, PAIRS, lanes), f32),
+            pltpu.VMEM((NB // 2 * ROWS, lanes), f32),
+            pltpu.VMEM((NB, ROWS // 8, 8, lanes), f32),
             pltpu.VMEM((ROWS, lanes), f32),
             pltpu.VMEM((PAIRS, 8, lanes), f32),
             pltpu.VMEM((ROWS, lanes), f32),
-            dma((4,)),
+            dma((8,)),
             dma((2, ITERS, RING - 1)),
             dma((2, ITERS, RING)),
             dma((2, ITERS, 2, RING)),
@@ -475,7 +523,7 @@
             dma((2, ITERS, 2, RING)),
         ],
         compiler_params=pltpu.CompilerParams(
-            collective_id=0, has_side_effects=True, vmem_limit_bytes=40 * 1024 * 1024
+            collective_id=0, has_side_effects=True, vmem_limit_bytes=63 * 1024 * 1024
         ),
     )(
         lesser, greater, retarded, coupling, offsets,

time: 83.3 us -> 72.5 us (0.87)
  Pallas kernels: 75.3 us -> 69.1 us
  local copies, waits for them, and re-layouts: 6.58 us -> 2.28 us
    pallas_call x1, Pallas kernels: 75.3 us -> 69.1 us  [body(): pl.pallas_call(kernel, out_shape=(jax.ShapeDtypeStruct(lesser.shape, f32)...]
    unnamed x18 -> x4, local copies, waits for them, and re-layouts: 6.58 us -> 2.28 us
where the time goes in v2:
time: 72.5 us; the launch traced here: 72 us
  Pallas kernels  69.1 us (95%)
  local copies, waits for them, and re-layouts  2.28 us (3%)
    pallas_call x1, Pallas kernels, body(): pl.pallas_call(kernel, out_shape=(jax.ShapeDtypeStruct(lesser.shape, f32)...  69.1 us
    unnamed x4, local copies, waits for them, and re-layouts  2.28 us

profile of v2, /device:TPU:1, one launch (start us, length us, event | category | flops | bytes accessed | tf_op | source)
XLA Modules:
  0.0 72.0 jit_solution(1169999902570077766)
XLA Ops:
  0.6 69.1 %shard_map.95 = (f32[2,144,128]{2,1,0:T(8,128)}, f32[2,144,128]{2,1,0:T(8,128)}) custom-call(f32[2,144,128]{2,1,0:T(8,128)} %lesser.1, f32[2,144,128]{2,1,0:T(8,128)} %greater.1, f32[2,144,128]{2,1,0:T(8,128)} %retarded.1, f32[12,144,128]{2,1,0:T(8,128)} %coupling.1, s32[12,128]{1,0:T(8,128)} %offsets_in.1, s32[1,64]{1,0:T(1,128)} %bitcast.3, ...), custom_call_target="tpu_custom_call" | custom-call | tf_op jit(solution)/shard_map/pallas_call | solution.py:482
  69.7 0.0 copy-start
  69.7 1.6 %copy.12 = f32[2,144,128]{2,1,0:T(8,128)} copy(f32[2,144,128]{2,1,0:T(8,128)} %get-tuple-element.4) | data formatting | bytes 294912
  71.4 0.0 copy-done
  71.4 0.7 copy.13
Async XLA Ops:
  69.7 1.6 %copy-start = (f32[2,144,128]{2,1,0:T(8,128)S(1)}, f32[2,144,128]{2,1,0:T(8,128)}, u32[]{:S(2)}) copy-start(f32[2,144,128]{2,1,0:T(8,128)} %get-tuple-element.5) | copy-start | bytes 442372

commit v3 on v2

--- a/solution.py
+++ b/solution.py
@@ -25,10 +25,6 @@
 
 def rows8(start):
     return pl.ds(start, 8)
-
-
-def pick(source, v, index):
-    return jnp.take_along_axis(source[rows8(8 * v), :], index, axis=1, mode="promise_in_bounds")
 
 
 def sandwich_step(n, links, wide_links, near, total):
@@ -94,7 +90,7 @@
     out_lesser, out_greater,
     offsets, shifts, strength, occupation, free_in, ret_in, links, wide_links, narrow_ret, wide_ret, taps, even_taps, odd_taps,
     lesser_buf, greater_buf, coupled, arrived, mixed, band, left_in, right_in,
-    pair_links, wide_pairs, stash, halo, total, sigma,
+    pair_links, wide_pairs, inner_hot, outer_hot, halves, stash, halo, total, sigma,
     load_sem, a1_send, a1_recv, z_send, z_recv, a2_send, a2_recv, x_send, x_recv,
 ):
     energy = lax.axis_index("energy")
@@ -286,16 +282,42 @@
             value = jnp.where(edge_ok, value, 0.0)
             halo[rows8(8 * v), :] = jnp.where(outer, value, half_turn(value))
 
+    def take_near(source, table, count):
+        value = source[pl.ds(0, ROWS), :]
+        high = value.astype(jnp.bfloat16)
+        halves[:, :LANES] = high
+        halves[:, LANES:] = (value - high.astype(jnp.float32)).astype(jnp.bfloat16)
+
+        for p in range(count):
+            found = jnp.dot(halves[...], table[p], preferred_element_type=jnp.float32)
+            stash[2 * p] = found[:, :LANES].reshape(ROWS // 8, 8, LANES)
+            stash[2 * p + 1] = found[:, LANES:].reshape(ROWS // 8, 8, LANES)
+
+    def mark(table, p, part, place):
+        wanted = jnp.concatenate([place] * (LANES // 8), axis=0)
+        row = lax.broadcasted_iota(jnp.int32, (LANES, LANES), 0)
+        hot = jnp.where(row == wanted, 1.0, 0.0).astype(jnp.bfloat16)
+        for copy in range(2):
+            table[p, copy * LANES : (copy + 1) * LANES, part * LANES : (part + 1) * LANES] = hot
+
+    def mark_inner(p, carry):
+        for part in range(2):
+            mark(inner_hot, p, part, lane + spread(offsets[pl.ds(2 * p + part, 1), :]))
+        return carry
+
+    def mark_outer(p, carry):
+        for part in range(2):
+            near = spread(offsets[pl.ds(4 * p + 2 * part, 1), :])
+            far = spread(offsets[pl.ds(4 * p + 2 * part + 1, 1), :])
+            atom = jnp.where(outer, lane, lane ^ (LANES // 2))
+            place = atom + jnp.where(outer, near, half_turn(far))
+            beyond = (place < 0) | (place >= LANES)
+            index = (place + jnp.where(outer, 0, LANES // 2)) & (LANES - 1)
+            mark(outer_hot, p, part, jnp.where(beyond, index, -1))
+        return carry
+
     def couple_own(own):
-        def one(n, carry):
-            place = lane + spread(offsets[pl.ds(n, 1), :])
-            inside = (place >= 0) & (place < LANES)
-            index = place & (LANES - 1)
-            for v in range(ROWS // 8):
-                stash[n, v] = jnp.where(inside, pick(own, v, index), 0.0)
-            return carry
-
-        lax.fori_loop(0, NB, one, 0)
+        take_near(own, inner_hot, NB // 2)
         total[...] = jnp.zeros(total.shape, jnp.float32)
 
     def couple_steps(begin, end):
@@ -314,18 +336,7 @@
                 target[rows8(8 * (3 * i + k3)), :] = folded(i, k3)
 
     def couple_halo(target):
-        def one(h, carry):
-            near = spread(offsets[pl.ds(2 * h, 1), :])
-            far = spread(offsets[pl.ds(2 * h + 1, 1), :])
-            atom = jnp.where(outer, lane, lane ^ (LANES // 2))
-            place = atom + jnp.where(outer, near, half_turn(far))
-            beyond = (place < 0) | (place >= LANES)
-            index = (place + jnp.where(outer, 0, LANES // 2)) & (LANES - 1)
-            for v in range(ROWS // 8):
-                stash[h, v] = jnp.where(beyond, pick(halo, v, index), 0.0)
-            return carry
-
-        lax.fori_loop(0, NB // 2, one, 0)
+        take_near(halo, outer_hot, NB // 4)
         total[...] = jnp.zeros(total.shape, jnp.float32)
 
         def step(h, carry):
@@ -403,12 +414,14 @@
         return carry
 
     lax.fori_loop(0, NB // 2, widen_pair, 0)
+    lax.fori_loop(0, NB // 2, mark_inner, 0)
     couple_own(greater_buf.at[0])
     couple_steps(0, NB)
     couple_inner(coupled.at[0])
+    spread_forward(0, 0)
+    lax.fori_loop(0, NB // 4, mark_outer, 0)
 
     def iteration(t, carry):
-        spread_forward(0, t)
         edges_finish(1, t)
         couple_halo(coupled.at[t])
         spread_start(1, t)
@@ -416,9 +429,9 @@
         spread_forward(1, t)
         collect(0, t, True)
         couple_own(arrived.at[0, t])
-        couple_steps(0, NB // 2)
+        couple_steps(0, NB // 4)
         mix(1, t)
-        couple_steps(NB // 2, NB)
+        couple_steps(NB // 4, NB)
         couple_inner(sigma)
         edges_finish(0, t)
         couple_halo(sigma)
@@ -437,6 +450,7 @@
             couple_own(greater_buf.at[t + 1])
             couple_steps(0, NB)
             couple_inner(coupled.at[t + 1])
+            spread_forward(0, t + 1)
 
         return carry
 
@@ -508,6 +522,9 @@
             pltpu.VMEM((2, ITERS, PADDED, lanes), f32),
             pltpu.VMEM((NB // 2, PAIRS, lanes), f32),
             pltpu.VMEM((NB // 2 * ROWS, lanes), f32),
+            pltpu.VMEM((NB // 2, 2 * lanes, 2 * lanes), jnp.bfloat16),
+            pltpu.VMEM((NB // 4, 2 * lanes, 2 * lanes), jnp.bfloat16),
+            pltpu.VMEM((ROWS, 2 * lanes), jnp.bfloat16),
             pltpu.VMEM((NB, ROWS // 8, 8, lanes), f32),
             pltpu.VMEM((ROWS, lanes), f32),
             pltpu.VMEM((PAIRS, 8, lanes), f32),

time: 72.5 us -> 69.7 us (0.961)
  Pallas kernels: 69.1 us -> 66.2 us
    pallas_call x1, Pallas kernels: 69.1 us -> 66.2 us  [body(): pl.pallas_call(kernel, out_shape=(jax.ShapeDtypeStruct(lesser.shape, f32)...]
where the time goes in v3:
time: 69.7 us; the launch traced here: 69.2 us
  Pallas kernels  66.2 us (95%)
  local copies, waits for them, and re-layouts  2.28 us (3%)
    pallas_call x1, Pallas kernels, body(): pl.pallas_call(kernel, out_shape=(jax.ShapeDtypeStruct(lesser.shape, f32)...  66.2 us
    unnamed x4, local copies, waits for them, and re-layouts  2.28 us

profile of v3, /device:TPU:1, one launch (start us, length us, event | category | flops | bytes accessed | tf_op | source)
XLA Modules:
  0.0 69.2 jit_solution(13782353728653342068)
XLA Ops:
  0.6 66.2 %shard_map.95 = (f32[2,144,128]{2,1,0:T(8,128)}, f32[2,144,128]{2,1,0:T(8,128)}) custom-call(f32[2,144,128]{2,1,0:T(8,128)} %lesser.1, f32[2,144,128]{2,1,0:T(8,128)} %greater.1, f32[2,144,128]{2,1,0:T(8,128)} %retarded.1, f32[12,144,128]{2,1,0:T(8,128)} %coupling.1, s32[12,128]{1,0:T(8,128)} %offsets_in.1, s32[1,64]{1,0:T(1,128)} %bitcast.3, ...), custom_call_target="tpu_custom_call" | custom-call | tf_op jit(solution)/shard_map/pallas_call | solution.py:496
  66.9 0.0 copy-start
  66.9 1.6 %copy.12 = f32[2,144,128]{2,1,0:T(8,128)} copy(f32[2,144,128]{2,1,0:T(8,128)} %get-tuple-element.4) | data formatting | bytes 294912
  68.5 0.0 copy-done
  68.5 0.7 copy.13
Async XLA Ops:
  66.9 1.6 %copy-start = (f32[2,144,128]{2,1,0:T(8,128)S(1)}, f32[2,144,128]{2,1,0:T(8,128)}, u32[]{:S(2)}) copy-start(f32[2,144,128]{2,1,0:T(8,128)} %get-tuple-element.5) | copy-start | bytes 442372

commit v4 on v3

--- a/solution.py
+++ b/solution.py
@@ -235,28 +235,23 @@
 
         lax.fori_loop(0, RING, blend, 0)
 
-    def collect(kind, t, forward):
+    def collect(kind, t):
         def take(m, carry):
             origin = (y + RING - hop(m) * (1 - m // (RING - 1))) % RING
             here = arrived.at[kind, t, piece(origin)]
             await_bytes(here, a2_recv.at[kind, t, m])
-            if forward:
-                remote(
-                    here, left_in.at[kind, t, piece(origin)],
-                    x_send.at[kind, t, 0, m], x_recv.at[kind, t, 0, m], (energy, right),
-                ).start()
-                remote(
-                    here, right_in.at[kind, t, piece(origin)],
-                    x_send.at[kind, t, 1, m], x_recv.at[kind, t, 1, m], (energy, left),
-                ).start()
             return carry
 
         lax.fori_loop(0, RING, take, 0)
 
-    def edges_start(t):
-        here = greater_buf.at[t]
-        remote(here, left_in.at[1, t], x_send.at[1, t, 0, 0], x_recv.at[1, t, 0, 0], (energy, right)).start()
-        remote(here, right_in.at[1, t], x_send.at[1, t, 1, 0], x_recv.at[1, t, 1, 0], (energy, left)).start()
+    whole = pl.ds(0, ROWS)
+
+    def edges_start(kind, held, t):
+        here = held.at[whole]
+        for side, (target, peer) in enumerate(((left_in, right), (right_in, left))):
+            remote(
+                here, target.at[kind, t, whole], x_send.at[kind, t, side], x_recv.at[kind, t, side], (energy, peer)
+            ).start()
 
     lane = lax.broadcasted_iota(jnp.int32, (8, LANES), 1)
     low_lanes = lane < LANES // 2
@@ -267,16 +262,8 @@
         return pltpu.roll(value, LANES // 2, 1)
 
     def edges_finish(kind, t):
-        if kind == 1:
-            await_bytes(left_in.at[1, t], x_recv.at[1, t, 0, 0])
-            await_bytes(right_in.at[1, t], x_recv.at[1, t, 1, 0])
-        else:
-            def arrive(m, carry):
-                for side in range(2):
-                    await_bytes(left_in.at[0, t, piece(0)], x_recv.at[0, t, side, m])
-                return carry
-
-            lax.fori_loop(0, RING, arrive, 0)
+        for side, target in enumerate((left_in, right_in)):
+            await_bytes(target.at[kind, t, whole], x_recv.at[kind, t, side])
         for v in range(ROWS // 8):
             value = jnp.where(low_lanes, right_in[kind, t, rows8(8 * v), :], left_in[kind, t, rows8(8 * v), :])
             value = jnp.where(edge_ok, value, 0.0)
@@ -368,7 +355,7 @@
 
     pl.semaphore_wait(barrier, RING + 3)
     spread_start(0, 0)
-    edges_start(0)
+    edges_start(1, greater_buf.at[0], 0)
 
     for load in loads[4:]:
         load.wait()
@@ -413,13 +400,13 @@
                 wide_pairs[pl.ds(h * ROWS + 16 * v + e, 8, stride=2), :] = value
         return carry
 
-    lax.fori_loop(0, NB // 2, widen_pair, 0)
     lax.fori_loop(0, NB // 2, mark_inner, 0)
     couple_own(greater_buf.at[0])
     couple_steps(0, NB)
     couple_inner(coupled.at[0])
     spread_forward(0, 0)
     lax.fori_loop(0, NB // 4, mark_outer, 0)
+    lax.fori_loop(0, NB // 2, widen_pair, 0)
 
     def iteration(t, carry):
         edges_finish(1, t)
@@ -427,11 +414,12 @@
         spread_start(1, t)
         mix(0, t)
         spread_forward(1, t)
-        collect(0, t, True)
+        collect(0, t)
+        edges_start(0, arrived.at[0, t], t)
         couple_own(arrived.at[0, t])
-        couple_steps(0, NB // 4)
+        couple_steps(0, 4)
         mix(1, t)
-        couple_steps(NB // 4, NB)
+        couple_steps(4, NB)
         couple_inner(sigma)
         edges_finish(0, t)
         couple_halo(sigma)
@@ -441,12 +429,12 @@
         def _():
             spread_start(0, t + 1)
 
-        collect(1, t, False)
+        collect(1, t)
         dress(arrived.at[1, t], greater_buf.at[0], greater_buf.at[t + 1], narrow_ret, wide_ret)
 
         @pl.when(t < ITERS - 1)
         def _():
-            edges_start(t + 1)
+            edges_start(1, greater_buf.at[t + 1], t + 1)
             couple_own(greater_buf.at[t + 1])
             couple_steps(0, NB)
             couple_inner(coupled.at[t + 1])
@@ -467,9 +455,6 @@
                 here = band.at[kind, t, piece(RING)]
                 for side in range(2):
                     await_bytes(here, z_send.at[kind, t, side, m])
-
-            for side in range(2):
-                await_bytes(arrived.at[0, t, piece(0)], x_send.at[0, t, side, m])
             return inner
 
         def sent(m, inner):
@@ -481,7 +466,8 @@
         lax.fori_loop(0, RING, pieces, 0)
         lax.fori_loop(0, RING - 1, sent, 0)
         for side in range(2):
-            await_bytes(greater_buf.at[t], x_send.at[1, t, side, 0])
+            for kind in range(2):
+                await_bytes(left_in.at[kind, t, whole], x_send.at[kind, t, side])
         return carry
 
     lax.fori_loop(0, ITERS, drain, 0)
@@ -536,8 +522,8 @@
             dma((2, ITERS, 2, RING)),
             dma((2, ITERS, RING - 1)),
             dma((2, ITERS, RING)),
-            dma((2, ITERS, 2, RING)),
-            dma((2, ITERS, 2, RING)),
+            dma((2, ITERS, 2)),
+            dma((2, ITERS, 2)),
         ],
         compiler_params=pltpu.CompilerParams(
             collective_id=0, has_side_effects=True, vmem_limit_bytes=63 * 1024 * 1024

time: 69.7 us -> 69.2 us (level)
  no operation moved by 1% of the time
where the time goes in v4:
time: 69.2 us; the launch traced here: 69.1 us
  Pallas kernels  66.1 us (96%)
  local copies, waits for them, and re-layouts  2.28 us (3%)
    pallas_call x1, Pallas kernels, body(): pl.pallas_call(kernel, out_shape=(jax.ShapeDtypeStruct(lesser.shape, f32)...  66.1 us
    unnamed x4, local copies, waits for them, and re-layouts  2.28 us

profile of v4, /device:TPU:1, one launch (start us, length us, event | category | flops | bytes accessed | tf_op | source)
XLA Modules:
  0.0 69.1 jit_solution(12065743388566427043)
XLA Ops:
  0.6 66.1 %shard_map.95 = (f32[2,144,128]{2,1,0:T(8,128)}, f32[2,144,128]{2,1,0:T(8,128)}) custom-call(f32[2,144,128]{2,1,0:T(8,128)} %lesser.1, f32[2,144,128]{2,1,0:T(8,128)} %greater.1, f32[2,144,128]{2,1,0:T(8,128)} %retarded.1, f32[12,144,128]{2,1,0:T(8,128)} %coupling.1, s32[12,128]{1,0:T(8,128)} %offsets_in.1, s32[1,64]{1,0:T(1,128)} %bitcast.3, ...), custom_call_target="tpu_custom_call" | custom-call | tf_op jit(solution)/shard_map/pallas_call | solution.py:482
  66.8 0.0 copy-start
  66.8 1.6 %copy.12 = f32[2,144,128]{2,1,0:T(8,128)} copy(f32[2,144,128]{2,1,0:T(8,128)} %get-tuple-element.4) | data formatting | bytes 294912
  68.4 0.0 copy-done
  68.4 0.7 copy.13
Async XLA Ops:
  66.8 1.6 %copy-start = (f32[2,144,128]{2,1,0:T(8,128)S(1)}, f32[2,144,128]{2,1,0:T(8,128)}, u32[]{:S(2)}) copy-start(f32[2,144,128]{2,1,0:T(8,128)} %get-tuple-element.5) | copy-start | bytes 442372
